TPU v7x, 1024 devices: a whole 4x8x16 slice. The times are simulated.
1024 devices in a mesh: pipe: 16 (over y, z_hi), tensor: 16 (over z_lo, core), dp: 4 (over x).
Axes of the slice: x: 4, y: 8, z: 16 (z_hi: 2, z_lo: 8; z = z_hi * 8 + z_lo), core: 2. Of those that a mesh axis runs over, the one named last changes fastest.
Arguments:
- out_grad: bfloat16 [16, 4, 128, 2560], P('pipe', 'dp', None, 'tensor'), may hold values from -6 to 6
- gate_pre: bfloat16 [16, 4, 13824, 128], P('pipe', 'dp', 'tensor'), may hold values from -6 to 6
- up_pre: bfloat16 [16, 4, 13824, 128], P('pipe', 'dp', 'tensor'), may hold values from -6 to 6
- down_weight: bfloat16 [16, 13824, 2560], P('pipe', 'tensor'), may hold values from -0.125 to 0.125
Outputs:
- gate_grad: bfloat16 [16, 4, 13824, 128], P('pipe', 'dp', 'tensor')
- up_grad: bfloat16 [16, 4, 13824, 128], P('pipe', 'dp', 'tensor')
- weight_grad: bfloat16 [16, 13824, 2560], P('pipe', 'tensor', 'dp')
All inputs are finite; a program needn't handle non-finite values.
Results may differ from a plain program's by a relative error of at most 0.0075.
Values may be sent and summed in bfloat16 or wider, within the bound.
A program may use at most 64 MiB of HBM per device.

v0:
```python
import jax
import jax.numpy as jnp
from jax import lax
from jax.sharding import PartitionSpec as P


def swapped(value, axis, bit):
    mask = 2**bit
    pairs = [(source, source ^ mask) for source in range(lax.axis_size(axis))]
    return lax.ppermute(value, axis, pairs)


def on_device(out_grad, gate_pre, up_pre, down_weight):
    grad_cols = lax.all_gather(out_grad, "tensor", axis=3, tiled=True)
    output_grad = grad_cols[0, 0]
    gate_vals = gate_pre[0, 0].astype(jnp.float32)
    up_vals = up_pre[0, 0].astype(jnp.float32)
    sigmoid_gate = jax.nn.sigmoid(gate_vals)
    silu_gate = gate_vals * sigmoid_gate
    hidden = (silu_gate * up_vals).astype(jnp.bfloat16)
    weight = down_weight[0]
    hidden_grad = lax.dot_general(
        weight, output_grad, (((1,), (1,)), ((), ())), preferred_element_type=jnp.float32
    )
    gate_grad = (
        hidden_grad * up_vals * sigmoid_gate * (1.0 + gate_vals * (1.0 - sigmoid_gate))
    ).astype(jnp.bfloat16)
    up_grad = (hidden_grad * silu_gate).astype(jnp.bfloat16)
    local_sum = jnp.dot(hidden, output_grad, preferred_element_type=jnp.float32)
    replica_sum = lax.psum_scatter(local_sum, "dp", scatter_dimension=1, tiled=True)
    pair_term = replica_sum.astype(jnp.bfloat16)
    top_bit = lax.axis_size("pipe").bit_length() - 2
    partner_term = swapped(pair_term, "pipe", top_bit)
    grad_scale = 32.0 / (2.0 * lax.axis_size("dp") * output_grad.shape[0])
    weight_grad = (
        (pair_term.astype(jnp.float32) + partner_term.astype(jnp.float32)) * grad_scale
    ).astype(jnp.bfloat16)
    return (gate_grad[None, None], up_grad[None, None], weight_grad[None])


def solution(mesh):
    in_specs = (
        P("pipe", "dp", None, "tensor"),
        P("pipe", "dp", "tensor", None),
        P("pipe", "dp", "tensor", None),
        P("pipe", "tensor", None),
    )
    out_specs = (
        P("pipe", "dp", "tensor", None),
        P("pipe", "dp", "tensor", None),
        P("pipe", "tensor", "dp"),
    )
    return jax.shard_map(
        on_device, mesh=mesh, in_specs=in_specs, out_specs=out_specs, check_vma=False
    )
```

profile of v0, /device:TPU:17, one launch (start us, length us, event | category | flops | bytes accessed | tf_op | source)
XLA Modules:
  0.0 216.6 jit_solution(14146861648869202700)
XLA Ops:
  7.2 0.0 reduce-scatter.2.cloned.1.call-start
  7.2 43.2 %all_gather.3 = bf16[1,1,128,2560]{2,3,1,0:T(8,128)(2,1)S(1)} all-gather(bf16[1,1,128,160]{2,3,1,0:T(8,128)(2,1)} %param.4), channel_id=1, replica_groups=mesh['pipe'=16,'tensor'=16,'dp'=4] {'tensor'}, dimensions={3}, use_global_device_ids=true | all-gather | bytes 696320 | tf_op jit(solution)/shard_map/all_gather | solution.py:14
  50.4 5.8 %fusion.6 = f32[864,2560]{1,0:T(8,128)} fusion(bf16[1,1,128,2560]{2,3,1,0:T(8,128)(2,1)S(1)} %all_gather.3, bf16[1,1,864,128]{3,2,1,0:T(8,128)(2,1)} %param.6, bf16[1,1,864,128]{3,2,1,0:T(8,128)(2,1)} %param.5), kind=kOutput, calls=%fused_computation.10 | convolution fusion | flops 567115776 | bytes 9945088 | tf_op jit(solution)/shard_map/dot_general | solution.py:29
  56.1 0.0 reduce-scatter.2.cloned.1.call-update
  56.2 0.0 copy-start.1
  56.2 0.0 copy-start.2
  56.2 94.6 %reduce-scatter.2.cloned.1.call-done = f32[864,640]{1,0:T(8,128)} async-done(((f32[864,2560]{1,0:T(8,128)}), f32[864,640]{1,0:T(8,128)}) %reduce-scatter.2.cloned.1.call-update) | async-done | bytes 2211856 | tf_op jit(solution)/shard_map/reduce_scatter | solution.py:30
  150.8 1.7 convert_element_type.52
  152.5 0.0 copy-start
  152.5 5.4 %collective-permute-start = (bf16[864,640]{1,0:T(8,128)(2,1)S(1)}, bf16[864,640]{1,0:T(8,128)(2,1)S(1)}, u32[]{:S(2)}, u32[]{:S(2)}) collective-permute-start(bf16[864,640]{1,0:T(8,128)(2,1)S(1)} %convert_element_type.52), channel_id=1, source_target_pairs={{0,512},{64,576},{128,640},{192,704},{256,768},{320,832},{384,896}... | collective-permute-start | bytes 3317768 | tf_op jit(solution)/shard_map/ppermute | solution.py:10
  158.0 0.0 copy-done.1
  158.0 0.0 copy-done.2
  158.0 4.3 %fusion.25 = (bf16[1,1,864,128]{3,2,1,0:T(8,128)(2,1)}, bf16[1,1,864,128]{3,2,1,0:T(8,128)(2,1)}) fusion(bf16[1,1,864,128]{3,2,1,0:T(8,128)(2,1)S(1)} %copy-done.1, bf16[1,1,864,128]{3,2,1,0:T(8,128)(2,1)S(1)} %copy-done.2, bf16[1,1,128,2560]{2,3,1,0:T(8,128)(2,1)S(1)} %all_gather.3, bf16[1,864,2560]{2,1,0:T(8,128)(2,1)} %param.7), kind=kOutput, calls=%fused_computation.30 | convolution fusion | flops 567889920 | bytes 5963776 | tf_op jit(solution)/shard_map/dot_general | solution.py:22
  162.3 46.2 %collective-permute-done = bf16[864,640]{1,0:T(8,128)(2,1)S(1)} collective-permute-done((bf16[864,640]{1,0:T(8,128)(2,1)S(1)}, bf16[864,640]{1,0:T(8,128)(2,1)S(1)}, u32[]{:S(2)}, u32[]{:S(2)}) %collective-permute-start) | collective-permute-done | bytes 1105952 | tf_op jit(solution)/shard_map/ppermute | solution.py:10
  208.5 0.0 copy-done
  208.5 1.3 fusion.2
Async XLA Ops:
  7.2 143.6 %reduce-scatter.2.cloned.1.call-start = ((), (), s32[]{:S(2)}) async-start(), calls=%async_computation.1 | async-start | bytes 11059200 | tf_op jit(solution)/shard_map/reduce_scatter | solution.py:30
  56.2 101.8 %copy-start.1 = (bf16[1,1,864,128]{3,2,1,0:T(8,128)(2,1)S(1)}, bf16[1,1,864,128]{3,2,1,0:T(8,128)(2,1)}, u32[]{:S(2)}) copy-start(bf16[1,1,864,128]{3,2,1,0:T(8,128)(2,1)} %param.5) | copy-start | bytes 663556
  56.2 101.8 %copy-start.2 = (bf16[1,1,864,128]{3,2,1,0:T(8,128)(2,1)S(1)}, bf16[1,1,864,128]{3,2,1,0:T(8,128)(2,1)}, u32[]{:S(2)}) copy-start(bf16[1,1,864,128]{3,2,1,0:T(8,128)(2,1)} %param.6) | copy-start | bytes 663556
  152.5 55.9 %copy-start = (f32[864,640]{1,0:T(8,128)S(1)}, f32[864,640]{1,0:T(8,128)}, u32[]{:S(2)}) copy-start(f32[864,640]{1,0:T(8,128)} %reduce-scatter.2.cloned.1.call-done) | copy-start | bytes 6635524
  152.5 55.9 %collective-permute-start = (bf16[864,640]{1,0:T(8,128)(2,1)S(1)}, bf16[864,640]{1,0:T(8,128)(2,1)S(1)}, u32[]{:S(2)}, u32[]{:S(2)}) collective-permute-start(bf16[864,640]{1,0:T(8,128)(2,1)S(1)} %convert_element_type.52), channel_id=1, source_target_pairs={{0,512},{64,576},{128,640},{192,704},{256,768},{320,832},{384,896}... | collective-permute-start | bytes 3317768 | tf_op jit(solution)/shard_map/ppermute | solution.py:10
Sparse Core Ops, SparseCore 0:
  56.3 94.4 reduce-scatter.1
where the time goes:
time: 217 us
  waiting for transfers between devices  141 us (65%)
  blocking collectives  43.2 us (20%)
  between operations  14.1 us (6%)
  matrix products  10.1 us (5%)
  starting transfers between devices  5.46 us (3%)
  other arithmetic  3.01 us (1%)
    reduce_scatter x1, waiting for transfers between devices, on_device(): lax.psum_scatter(local_sum, 'dp', scatter_dimension=1, tiled=True)  94.6 us
    ppermute x1, waiting for transfers between devices, swapped(): return lax.ppermute(value, axis, pairs)  46.2 us
    all_gather x1, blocking collectives, on_device(): grad_cols = lax.all_gather(out_grad, 'tensor', axis=3, tiled=True)  43.2 us
    dot_general x1, matrix products, on_device(): local_sum = jnp.dot(hidden, output_grad, preferred_element_type=jnp.float32)  5.78 us
    ppermute x1, starting transfers between devices, swapped(): return lax.ppermute(value, axis, pairs)  5.42 us
  transfers between devices with their start and end apart: 2, of which 2 were waited for; matrix products, arithmetic and copies ran while one was open for 2% of the time, Pallas kernels for 0%

commit v1 on v0

v1 whole, which is shorter than its diff:
```python
import functools

import jax
import jax.numpy as jnp
from jax import lax
from jax.experimental import pallas as pl
from jax.experimental.pallas import tpu as pltpu
from jax.sharding import PartitionSpec as P

MESH = pl.DeviceIdType.MESH
CHUNKS = 3


def kernel(
    sizes,
    og_hbm, gate_hbm, up_hbm, weight_hbm,
    gg_hbm, ug_hbm, wg_hbm,
    og_in, gate, up, weight, og_all, wog, hid, acc, gg, ug, wg,
    local_sem, out_sem, og_send, og_recv, wog_send, wog_recv, hid_send, hid_recv,
):
    n_pipe, n_tensor, n_dp, rows, tok, width, scale = sizes
    p, t, x = lax.axis_index("pipe"), lax.axis_index("tensor"), lax.axis_index("dp")
    n_class = n_tensor // 4
    u, zr = lax.rem(t, 4), t // 4
    core = lax.rem(t, 2)
    sib = (p, t + 1 - 2 * core, x)
    near = (p, t + 2 - 4 * (u // 2), x)
    mirror = (lax.rem(p + n_pipe // 2, n_pipe), t, x)
    right = (p, t, lax.rem(x + 1, n_dp))
    left = (p, t, lax.rem(x + n_dp - 1, n_dp))
    across = (p, t, lax.rem(x + 2, n_dp))
    u_sib = u + 1 - 2 * core
    u_near = u + 2 - 4 * (u // 2)
    u_far = u_near + 1 - 2 * core
    mates = [lax.rem(zr + i, n_class) for i in range(n_class)]
    step = rows // CHUNKS
    half = step // 2

    loads = [
        pltpu.make_async_copy(og_hbm.at[0, 0], og_in, local_sem.at[0]),
        pltpu.make_async_copy(gate_hbm.at[0, 0], gate, local_sem.at[1]),
        pltpu.make_async_copy(up_hbm.at[0, 0], up, local_sem.at[2]),
        pltpu.make_async_copy(weight_hbm.at[0], weight, local_sem.at[3]),
    ]
    for load in loads:
        load.start()

    barrier = pltpu.get_barrier_semaphore()
    greeted = [sib, near, mirror, right, left, across] + [
        (p, 4 * r + u, x) for r in mates[1:]
    ]
    for device in greeted:
        pl.semaphore_signal(barrier, inc=1, device_id=device, device_id_type=MESH)

    def remote(src, dst, send, recv, device):
        return pltpu.make_async_remote_copy(
            src_ref=src, dst_ref=dst, send_sem=send, recv_sem=recv,
            device_id=device, device_id_type=MESH,
        )

    sent = []

    def send(src, dst, send_sem, recv_sem, device):
        copy = remote(src, dst, send_sem, recv_sem, device)
        copy.start()
        sent.append(copy)

    loads[0].wait()
    og_all[t] = og_in[...]

    loads[1].wait()
    loads[2].wait()

    def hidden_rows(i, carry):
        at = pl.ds(pl.multiple_of(i * half, half), half)
        g = gate[at, :].astype(jnp.float32)
        v = up[at, :].astype(jnp.float32)
        hid[0, 0, at, :] = (g * jax.nn.sigmoid(g) * v).astype(jnp.bfloat16)
        return carry

    lax.fori_loop(0, 2 * CHUNKS, hidden_rows, 0)

    pl.semaphore_wait(barrier, len(greeted))

    og_count = [0]

    def send_og(shard, device):
        n = og_count[0]
        og_count[0] += 1
        send(og_all.at[shard], og_all.at[shard], og_send.at[n], og_recv.at[shard], device)

    def wait_og(shard):
        remote(og_all.at[shard], og_all.at[shard], og_send.at[0], og_recv.at[shard], sib).wait_recv()

    wog_count = [0]

    def send_wog(q, k, v, src, q_to, device):
        n = wog_count[0]
        wog_count[0] += 1
        send(src, wog.at[q_to, k, v], wog_send.at[n], wog_recv.at[q_to, k, v], device)

    def wait_wog(q, k, v):
        remote(wog.at[q, k, v], wog.at[q, k, v], wog_send.at[0], wog_recv.at[q, k, v], sib).wait_recv()

    hid_count = [0]

    def send_hid(q, k, q_to, k_to, first, count, device):
        n = hid_count[0]
        hid_count[0] += 1
        at = pl.ds(first * half, count * half)
        send(
            hid.at[q, k, at], hid.at[q_to, k_to, at],
            hid_send.at[n], hid_recv.at[q_to, k_to, first], device,
        )

    def wait_hid(q, k, first, count):
        at = pl.ds(first * half, count * half)
        remote(
            hid.at[q, k, at], hid.at[q, k, at],
            hid_send.at[0], hid_recv.at[q, k, first], sib,
        ).wait_recv()

    def route_block(r):
        n = wog_count[0]
        wog_count[0] += 1
        shard = 4 * r + u
        k = lax.rem(x - r + n_dp, n_dp)

        @pl.when(r == x)
        def _():
            remote(og_all.at[shard], wog.at[1, 0, u], wog_send.at[n], wog_recv.at[1, 0, u], mirror).start()

        @pl.when(r != x)
        def _():
            remote(og_all.at[shard], wog.at[0, k, u], wog_send.at[n], wog_recv.at[0, k, u], (p, t, r)).start()

        sent.append(remote(og_all.at[shard], wog.at[0, 0, u], wog_send.at[n], wog_recv.at[0, 0, u], mirror))

    def take_mate(i):
        r = mates[i]
        if i:
            wait_og(4 * r + u)
        route_block(r)
        send_og(4 * r + u, near)
        send_og(4 * r + u, sib)

    def own_hidden(c):
        send_hid(0, 0, 0, n_dp - 1, 2 * c, 2, right)
        send_hid(0, 0, 0, 1, 2 * c, 2, left)
        send_hid(0, 0, 1, 0, 2 * c, 2, mirror)

    def relay_ring(q, c):
        wait_hid(q, 3, 2 * c, 2)
        send_hid(q, 3, q, 2, 2 * c, 1, right)
        wait_hid(q, 1, 2 * c, 2)
        send_hid(q, 1, q, 2, 2 * c + 1, 1, left)

    def relay_mirror(c):
        wait_hid(1, 0, 2 * c, 2)
        send_hid(1, 0, 1, n_dp - 1, 2 * c, 2, right)
        send_hid(1, 0, 1, 1, 2 * c, 2, left)

    for i in range(1, n_class):
        send_og(4 * zr + u, (p, 4 * mates[i] + u, x))
    take_mate(0)
    for c in range(CHUNKS):
        own_hidden(c)

    relay_ring(0, 0)
    take_mate(1)
    relay_ring(0, 1)
    take_mate(2)
    relay_ring(0, 2)
    relay_mirror(0)
    take_mate(3)
    for k in range(1, n_dp):
        wait_wog(0, k, u)
        send_wog(0, k, u, wog.at[0, k, u], 1, mirror)
        send_wog(0, k, u, wog.at[0, k, u], 0, near)
        send_wog(0, k, u, wog.at[0, k, u], 0, sib)
    relay_ring(1, 0)
    relay_mirror(1)
    for r in range(n_class):
        wait_og(4 * r + u_near)
        send_og(4 * r + u_near, sib)
    for k in range(1, n_dp):
        wait_wog(0, k, u_near)
        send_wog(0, k, u_near, wog.at[0, k, u_near], 0, sib)
    relay_ring(1, 1)
    relay_mirror(2)
    for r in range(n_class):
        wait_og(4 * r + u_sib)
        wait_og(4 * r + u_far)

    loads[3].wait()

    def projection_rows(i, carry):
        at = pl.ds(pl.multiple_of(i * half, half), half)
        grad = jnp.dot(
            weight[at, :], og_all[...].reshape(n_tensor * width, tok),
            preferred_element_type=jnp.float32,
        )
        g = gate[at, :].astype(jnp.float32)
        v = up[at, :].astype(jnp.float32)
        s = jax.nn.sigmoid(g)
        gg[at, :] = (grad * v * s * (1.0 + g * (1.0 - s))).astype(jnp.bfloat16)
        ug[at, :] = (grad * g * s).astype(jnp.bfloat16)
        return carry

    lax.fori_loop(0, 2 * CHUNKS, projection_rows, 0)
    outs = [
        pltpu.make_async_copy(gg, gg_hbm.at[0, 0], out_sem.at[0]),
        pltpu.make_async_copy(ug, ug_hbm.at[0, 0], out_sem.at[1]),
    ]
    for out in outs:
        out.start()

    for k in range(n_dp):
        wait_wog(1, k, u)
        send_wog(1, k, u, wog.at[1, k, u], 1, near)
        send_wog(1, k, u, wog.at[1, k, u], 1, sib)
    relay_ring(1, 2)

    for k in range(1, n_dp):
        wait_wog(0, k, u_sib)
        wait_wog(0, k, u_far)
    for first in range(2 * CHUNKS):
        wait_hid(0, 2, first, 1)

    def block_of(q, k):
        if q == 0 and k == 0:
            return og_all[pl.ds(4 * x, 4)].reshape(4 * width, tok)
        return wog[q, k].reshape(4 * width, tok)

    def term(q, at):
        left_side = jnp.concatenate([hid[q, k, at, :] for k in range(n_dp)], axis=1)
        right_side = jnp.concatenate([block_of(q, k) for k in range(n_dp)], axis=1)
        return lax.dot_general(
            left_side, right_side, (((1,), (1,)), ((), ())), preferred_element_type=jnp.float32
        )

    def own_rows(i, carry):
        at = pl.ds(pl.multiple_of(i * half, half), half)
        acc[at, :] = term(0, at)
        return carry

    lax.fori_loop(0, 2 * CHUNKS, own_rows, 0)

    for k in range(n_dp):
        wait_wog(1, k, u_near)
        send_wog(1, k, u_near, wog.at[1, k, u_near], 1, sib)
    for k in range(n_dp):
        wait_wog(1, k, u_sib)
        wait_wog(1, k, u_far)

    for c in range(CHUNKS):
        wait_hid(1, 2, 2 * c, 1)
        wait_hid(1, 2, 2 * c + 1, 1)

        def mirror_rows(i, carry):
            at = pl.ds(pl.multiple_of(i * half, half), half)
            wg[at, :] = ((acc[at, :] + term(1, at)) * scale).astype(jnp.bfloat16)
            return carry

        lax.fori_loop(2 * c, 2 * c + 2, mirror_rows, 0)
        at = pl.ds(c * step, step)
        out = pltpu.make_async_copy(wg.at[at], wg_hbm.at[0, at], out_sem.at[2 + c])
        out.start()
        outs.append(out)

    for copy in sent:
        copy.wait_send()
    for out in outs:
        out.wait()


def solution(mesh):
    n_pipe, n_tensor, n_dp = mesh.shape["pipe"], mesh.shape["tensor"], mesh.shape["dp"]

    def on_device(out_grad, gate_pre, up_pre, down_weight):
        tok, width = out_grad.shape[2:]
        rows = gate_pre.shape[2]
        full = down_weight.shape[2]
        cols = full // n_dp
        scale = 32.0 / (2.0 * n_dp * tok)
        sizes = (n_pipe, n_tensor, n_dp, rows, tok, width, scale)
        bf16, f32 = jnp.bfloat16, jnp.float32
        any_space = pl.BlockSpec(memory_space=pl.ANY)
        dma = pltpu.SemaphoreType.DMA
        return pl.pallas_call(
            functools.partial(kernel, sizes),
            out_shape=(
                jax.ShapeDtypeStruct((1, 1, rows, tok), bf16),
                jax.ShapeDtypeStruct((1, 1, rows, tok), bf16),
                jax.ShapeDtypeStruct((1, rows, cols), bf16),
            ),
            in_specs=[any_space] * 4,
            out_specs=(any_space,) * 3,
            scratch_shapes=[
                pltpu.VMEM((width, tok), bf16),
                pltpu.VMEM((rows, tok), bf16),
                pltpu.VMEM((rows, tok), bf16),
                pltpu.VMEM((rows, full), bf16),
                pltpu.VMEM((n_tensor, width, tok), bf16),
                pltpu.VMEM((2, n_dp, 4, width, tok), bf16),
                pltpu.VMEM((2, n_dp, rows, tok), bf16),
                pltpu.VMEM((rows, cols), f32),
                pltpu.VMEM((rows, tok), bf16),
                pltpu.VMEM((rows, tok), bf16),
                pltpu.VMEM((rows, cols), bf16),
                dma((4,)),
                dma((2 + CHUNKS,)),
                dma((16,)),
                dma((n_tensor,)),
                dma((40,)),
                dma((2, n_dp, 4)),
                dma((36,)),
                dma((2, n_dp, 2 * CHUNKS)),
            ],
            compiler_params=pltpu.CompilerParams(
                collective_id=0, has_side_effects=True, vmem_limit_bytes=60 * 2**20
            ),
        )(jnp.swapaxes(out_grad, 2, 3), gate_pre, up_pre, down_weight)

    in_specs = (
        P("pipe", "dp", None, "tensor"),
        P("pipe", "dp", "tensor", None),
        P("pipe", "dp", "tensor", None),
        P("pipe", "tensor", None),
    )
    out_specs = (
        P("pipe", "dp", "tensor", None),
        P("pipe", "dp", "tensor", None),
        P("pipe", "tensor", "dp"),
    )
    return jax.shard_map(
        on_device, mesh=mesh, in_specs=in_specs, out_specs=out_specs, check_vma=False
    )
```

time: 217 us -> 56.4 us (0.26)
  the two profiles are of different devices: /device:TPU:17 before, /device:TPU:1 now
where the time goes in v1:
time: 56.4 us; the launch traced here: 56.1 us
  Pallas kernels  49.9 us (88%)
  local copies, waits for them, and re-layouts  5.6 us (10%)
  between operations  0.64 us (1%)
    pallas_call x1, Pallas kernels, on_device(): pl.pallas_call(functools.partial(kernel, sizes), out_shape=(jax.ShapeDtyp...  49.9 us
    unnamed x3, local copies, waits for them, and re-layouts  5.6 us

profile of v1, /device:TPU:1, one launch (start us, length us, event | category | flops | bytes accessed | tf_op | source)
XLA Modules:
  0.0 56.1 jit_solution(5703086622184534634)
XLA Ops:
  0.6 49.9 %shard_map.67 = (bf16[1,1,864,128]{3,2,1,0:T(8,128)(2,1)}, bf16[1,1,864,128]{3,2,1,0:T(8,128)(2,1)}, bf16[1,864,640]{2,1,0:T(8,128)(2,1)}) custom-call(bf16[1,1,160,128]{3,2,1,0:T(8,128)(2,1)} %bitcast.1, bf16[1,1,864,128]{3,2,1,0:T(8,128)(2,1)} %gate_hbm.1, bf16[1,1,864,128]{3,2,1,0:T(8,128)(2,1)} %up_hbm.1, bf16[1,864,2560]{2,1,0:T(8,128)(2,1)} %weight_hbm.1), custom_call_target="tpu_custom_call" | custom-call | tf_op jit(solution)/shard_map/pallas_call | solution.py:290
  50.5 1.6 %copy.10 = bf16[1,1,864,128]{3,2,1,0:T(8,128)(2,1)} copy(bf16[1,1,864,128]{3,2,1,0:T(8,128)(2,1)} %get-tuple-element.6) | data formatting | bytes 442368
  52.2 1.6 %copy.11 = bf16[1,1,864,128]{3,2,1,0:T(8,128)(2,1)} copy(bf16[1,1,864,128]{3,2,1,0:T(8,128)(2,1)} %get-tuple-element.7) | data formatting | bytes 442368
  53.8 2.3 %copy.12 = bf16[1,864,640]{2,1,0:T(8,128)(2,1)} copy(bf16[1,864,640]{2,1,0:T(8,128)(2,1)} %get-tuple-element.8) | data formatting | bytes 2211840

commit v2 on v1

--- a/solution.py
+++ b/solution.py
@@ -14,9 +14,9 @@
 def kernel(
     sizes,
     og_hbm, gate_hbm, up_hbm, weight_hbm,
-    gg_hbm, ug_hbm, wg_hbm,
-    og_in, gate, up, weight, og_all, wog, hid, acc, gg, ug, wg,
-    local_sem, out_sem, og_send, og_recv, wog_send, wog_recv, hid_send, hid_recv,
+    gg, ug, wg,
+    og_in, gate, up, weight, og_all, wog, hid, acc,
+    local_sem, og_send, og_recv, block_send, wog_send, wog_recv, hid_send, hid_recv, ready,
 ):
     n_pipe, n_tensor, n_dp, rows, tok, width, scale = sizes
     p, t, x = lax.axis_index("pipe"), lax.axis_index("tensor"), lax.axis_index("dp")
@@ -28,11 +28,11 @@
     mirror = (lax.rem(p + n_pipe // 2, n_pipe), t, x)
     right = (p, t, lax.rem(x + 1, n_dp))
     left = (p, t, lax.rem(x + n_dp - 1, n_dp))
-    across = (p, t, lax.rem(x + 2, n_dp))
+    ring = [(p, t, lax.rem(x + i, n_dp)) for i in range(1, n_dp)]
+    mirror_ring = [(mirror[0], t, lax.rem(x + i, n_dp)) for i in range(1, n_dp)]
     u_sib = u + 1 - 2 * core
     u_near = u + 2 - 4 * (u // 2)
     u_far = u_near + 1 - 2 * core
-    mates = [lax.rem(zr + i, n_class) for i in range(n_class)]
     step = rows // CHUNKS
     half = step // 2
 
@@ -45,12 +45,26 @@
     for load in loads:
         load.start()
 
+    def signal(sem, device):
+        pl.semaphore_signal(sem, inc=1, device_id=device, device_id_type=MESH)
+
+    def mate(r):
+        return (p, 4 * r + u, x)
+
+    near_above = u < 2
     barrier = pltpu.get_barrier_semaphore()
-    greeted = [sib, near, mirror, right, left, across] + [
-        (p, 4 * r + u, x) for r in mates[1:]
-    ]
-    for device in greeted:
-        pl.semaphore_signal(barrier, inc=1, device_id=device, device_id_type=MESH)
+    level = [sib, mirror] + ring + mirror_ring
+    for device in level:
+        signal(barrier, device)
+
+    @pl.when(near_above)
+    def _():
+        signal(barrier, near)
+
+    for r in range(n_class):
+        @pl.when(r > zr)
+        def _(r=r):
+            signal(barrier, mate(r))
 
     def remote(src, dst, send, recv, device):
         return pltpu.make_async_remote_copy(
@@ -80,17 +94,22 @@
 
     lax.fori_loop(0, 2 * CHUNKS, hidden_rows, 0)
 
-    pl.semaphore_wait(barrier, len(greeted))
-
-    og_count = [0]
-
-    def send_og(shard, device):
-        n = og_count[0]
-        og_count[0] += 1
-        send(og_all.at[shard], og_all.at[shard], og_send.at[n], og_recv.at[shard], device)
+    pl.semaphore_wait(barrier, len(level) + u // 2 + zr)
+
+    @pl.when(jnp.logical_not(near_above))
+    def _():
+        signal(ready.at[n_class], near)
+
+    for r in range(n_class):
+        @pl.when(r < zr)
+        def _(r=r):
+            signal(ready.at[zr], mate(r))
+
+    def og_copy(shard, n, device):
+        return remote(og_all.at[shard], og_all.at[shard], og_send.at[n], og_recv.at[shard], device)
 
     def wait_og(shard):
-        remote(og_all.at[shard], og_all.at[shard], og_send.at[0], og_recv.at[shard], sib).wait_recv()
+        og_copy(shard, 0, sib).wait_recv()
 
     wog_count = [0]
 
@@ -120,34 +139,63 @@
             hid_send.at[0], hid_recv.at[q, k, first], sib,
         ).wait_recv()
 
-    def route_block(r):
-        n = wog_count[0]
-        wog_count[0] += 1
+    def block_copies(r, n):
         shard = 4 * r + u
         k = lax.rem(x - r + n_dp, n_dp)
-
-        @pl.when(r == x)
-        def _():
-            remote(og_all.at[shard], wog.at[1, 0, u], wog_send.at[n], wog_recv.at[1, 0, u], mirror).start()
+        return [
+            remote(
+                og_all.at[shard], wog.at[q, k, u], block_send.at[q, n], wog_recv.at[q, k, u],
+                (lax.rem(p + q * (n_pipe // 2), n_pipe), t, r),
+            )
+            for q in range(2)
+        ]
+
+    def share(r, n):
+        here, there = block_copies(r, n)
 
         @pl.when(r != x)
         def _():
-            remote(og_all.at[shard], wog.at[0, k, u], wog_send.at[n], wog_recv.at[0, k, u], (p, t, r)).start()
-
-        sent.append(remote(og_all.at[shard], wog.at[0, 0, u], wog_send.at[n], wog_recv.at[0, 0, u], mirror))
-
-    def take_mate(i):
-        r = mates[i]
-        if i:
+            here.start()
+
+        there.start()
+        og_copy(4 * r + u, 3 * n, sib).start()
+
+    def offer(d, when):
+        r, n = zr + d, 3 + d
+
+        @pl.when((r < n_class) & when)
+        def _():
+            pl.semaphore_wait(ready.at[r], 1)
+            og_copy(4 * zr + u, 3 * n + 1, mate(r)).start()
+
+    def take(d, when=True):
+        r, n = zr + d, 3 + d
+
+        @pl.when((r >= 0) & (r < n_class) & when)
+        def _():
             wait_og(4 * r + u)
-        route_block(r)
-        send_og(4 * r + u, near)
-        send_og(4 * r + u, sib)
+            share(r, n)
+            og_copy(4 * r + u, 3 * n + 2, near).start()
+
+    def took(d):
+        r, n = zr + d, 3 + d
+
+        @pl.when((r >= 0) & (r < n_class))
+        def _():
+            here, there = block_copies(r, n)
+
+            @pl.when(r != x)
+            def _():
+                here.wait_send()
+
+            there.wait_send()
+            for i in range(2 if d == 0 else 3):
+                og_copy(4 * r + u, 3 * n + (2 * i if d == 0 else i), sib).wait_send()
 
     def own_hidden(c):
+        send_hid(0, 0, 1, 0, 2 * c, 2, mirror)
         send_hid(0, 0, 0, n_dp - 1, 2 * c, 2, right)
         send_hid(0, 0, 0, 1, 2 * c, 2, left)
-        send_hid(0, 0, 1, 0, 2 * c, 2, mirror)
 
     def relay_ring(q, c):
         wait_hid(q, 3, 2 * c, 2)
@@ -160,38 +208,65 @@
         send_hid(1, 0, 1, n_dp - 1, 2 * c, 2, right)
         send_hid(1, 0, 1, 1, 2 * c, 2, left)
 
-    for i in range(1, n_class):
-        send_og(4 * zr + u, (p, 4 * mates[i] + u, x))
-    take_mate(0)
+    for d in range(1 - n_class, 0):
+        @pl.when(zr + d >= 0)
+        def _(d=d):
+            og_copy(4 * zr + u, 3 * (3 + d) + 1, mate(zr + d)).start()
+
+    share(zr, 3)
     for c in range(CHUNKS):
         own_hidden(c)
 
+    @pl.when(near_above)
+    def _():
+        pl.semaphore_wait(ready.at[n_class], 1)
+
+    og_copy(4 * zr + u, 3 * 3 + 2, near).start()
+
+    def relay_block(q, v):
+        for k in range(1 - q, n_dp):
+            wait_wog(q, k, v)
+            if v is u:
+                send_wog(q, k, v, wog.at[q, k, v], q, near)
+            send_wog(q, k, v, wog.at[q, k, v], q, sib)
+
+    together = lax.rem(p, 2) == 1
+    apart = jnp.logical_not(together)
+
+    for d in range(1, n_class):
+        offer(d, together)
     relay_ring(0, 0)
-    take_mate(1)
+    take(-1)
+    offer(1, apart)
+    take(1, together)
     relay_ring(0, 1)
-    take_mate(2)
+    take(-2)
+    take(2, together)
+    take(1, apart)
+    relay_mirror(0)
     relay_ring(0, 2)
-    relay_mirror(0)
-    take_mate(3)
-    for k in range(1, n_dp):
-        wait_wog(0, k, u)
-        send_wog(0, k, u, wog.at[0, k, u], 1, mirror)
-        send_wog(0, k, u, wog.at[0, k, u], 0, near)
-        send_wog(0, k, u, wog.at[0, k, u], 0, sib)
+    offer(2, apart)
+    take(-3)
+    take(3, together)
     relay_ring(1, 0)
     relay_mirror(1)
+    take(2, apart)
+    offer(3, apart)
+    relay_ring(1, 1)
+    relay_mirror(2)
+    take(3, apart)
+    relay_block(0, u)
     for r in range(n_class):
         wait_og(4 * r + u_near)
-        send_og(4 * r + u_near, sib)
-    for k in range(1, n_dp):
-        wait_wog(0, k, u_near)
-        send_wog(0, k, u_near, wog.at[0, k, u_near], 0, sib)
-    relay_ring(1, 1)
-    relay_mirror(2)
+        n = 3 * (2 * n_class - 1) + r
+        og_copy(4 * r + u_near, n, sib).start()
+        sent.append(og_copy(4 * r + u_near, n, sib))
+    relay_block(1, u)
+    relay_block(0, u_near)
+
     for r in range(n_class):
         wait_og(4 * r + u_sib)
         wait_og(4 * r + u_far)
-
     loads[3].wait()
 
     def projection_rows(i, carry):
@@ -203,23 +278,14 @@
         g = gate[at, :].astype(jnp.float32)
         v = up[at, :].astype(jnp.float32)
         s = jax.nn.sigmoid(g)
-        gg[at, :] = (grad * v * s * (1.0 + g * (1.0 - s))).astype(jnp.bfloat16)
-        ug[at, :] = (grad * g * s).astype(jnp.bfloat16)
+        gg[0, 0, at, :] = (grad * v * s * (1.0 + g * (1.0 - s))).astype(jnp.bfloat16)
+        ug[0, 0, at, :] = (grad * g * s).astype(jnp.bfloat16)
         return carry
 
     lax.fori_loop(0, 2 * CHUNKS, projection_rows, 0)
-    outs = [
-        pltpu.make_async_copy(gg, gg_hbm.at[0, 0], out_sem.at[0]),
-        pltpu.make_async_copy(ug, ug_hbm.at[0, 0], out_sem.at[1]),
-    ]
-    for out in outs:
-        out.start()
-
-    for k in range(n_dp):
-        wait_wog(1, k, u)
-        send_wog(1, k, u, wog.at[1, k, u], 1, near)
-        send_wog(1, k, u, wog.at[1, k, u], 1, sib)
+
     relay_ring(1, 2)
+    relay_block(1, u_near)
 
     for k in range(1, n_dp):
         wait_wog(0, k, u_sib)
@@ -247,9 +313,6 @@
     lax.fori_loop(0, 2 * CHUNKS, own_rows, 0)
 
     for k in range(n_dp):
-        wait_wog(1, k, u_near)
-        send_wog(1, k, u_near, wog.at[1, k, u_near], 1, sib)
-    for k in range(n_dp):
         wait_wog(1, k, u_sib)
         wait_wog(1, k, u_far)
 
@@ -259,19 +322,24 @@
 
         def mirror_rows(i, carry):
             at = pl.ds(pl.multiple_of(i * half, half), half)
-            wg[at, :] = ((acc[at, :] + term(1, at)) * scale).astype(jnp.bfloat16)
+            wg[0, at, :] = ((acc[at, :] + term(1, at)) * scale).astype(jnp.bfloat16)
             return carry
 
         lax.fori_loop(2 * c, 2 * c + 2, mirror_rows, 0)
-        at = pl.ds(c * step, step)
-        out = pltpu.make_async_copy(wg.at[at], wg_hbm.at[0, at], out_sem.at[2 + c])
-        out.start()
-        outs.append(out)
 
     for copy in sent:
         copy.wait_send()
-    for out in outs:
-        out.wait()
+    for d in range(1 - n_class, n_class):
+        took(d)
+
+
+def write_out(gg, ug, wg, gg_out, ug_out, wg_out, sem):
+    pairs = ((gg, gg_out), (ug, ug_out), (wg, wg_out))
+    copies = [pltpu.make_async_copy(a, b, sem.at[i]) for i, (a, b) in enumerate(pairs)]
+    for copy in copies:
+        copy.start()
+    for copy in copies:
+        copy.wait()
 
 
 def solution(mesh):
@@ -285,17 +353,18 @@
         scale = 32.0 / (2.0 * n_dp * tok)
         sizes = (n_pipe, n_tensor, n_dp, rows, tok, width, scale)
         bf16, f32 = jnp.bfloat16, jnp.float32
-        any_space = pl.BlockSpec(memory_space=pl.ANY)
+        hbm = pl.BlockSpec(memory_space=pltpu.HBM)
+        vmem = pl.BlockSpec(memory_space=pltpu.VMEM)
         dma = pltpu.SemaphoreType.DMA
-        return pl.pallas_call(
+        grads = pl.pallas_call(
             functools.partial(kernel, sizes),
             out_shape=(
-                jax.ShapeDtypeStruct((1, 1, rows, tok), bf16),
-                jax.ShapeDtypeStruct((1, 1, rows, tok), bf16),
-                jax.ShapeDtypeStruct((1, rows, cols), bf16),
+                pltpu.VMEM((1, 1, rows, tok), bf16),
+                pltpu.VMEM((1, 1, rows, tok), bf16),
+                pltpu.VMEM((1, rows, cols), bf16),
             ),
-            in_specs=[any_space] * 4,
-            out_specs=(any_space,) * 3,
+            in_specs=[hbm] * 4,
+            out_specs=(vmem,) * 3,
             scratch_shapes=[
                 pltpu.VMEM((width, tok), bf16),
                 pltpu.VMEM((rows, tok), bf16),
@@ -305,22 +374,28 @@
                 pltpu.VMEM((2, n_dp, 4, width, tok), bf16),
                 pltpu.VMEM((2, n_dp, rows, tok), bf16),
                 pltpu.VMEM((rows, cols), f32),
-                pltpu.VMEM((rows, tok), bf16),
-                pltpu.VMEM((rows, tok), bf16),
-                pltpu.VMEM((rows, cols), bf16),
                 dma((4,)),
-                dma((2 + CHUNKS,)),
-                dma((16,)),
+                dma((26,)),
                 dma((n_tensor,)),
-                dma((40,)),
+                dma((2, 7)),
+                dma((24,)),
                 dma((2, n_dp, 4)),
                 dma((36,)),
                 dma((2, n_dp, 2 * CHUNKS)),
+                pltpu.SemaphoreType.REGULAR((5,)),
             ],
             compiler_params=pltpu.CompilerParams(
                 collective_id=0, has_side_effects=True, vmem_limit_bytes=60 * 2**20
             ),
         )(jnp.swapaxes(out_grad, 2, 3), gate_pre, up_pre, down_weight)
+        return pl.pallas_call(
+            write_out,
+            out_shape=[jax.ShapeDtypeStruct(g.shape, g.dtype) for g in grads],
+            in_specs=[pl.BlockSpec(memory_space=pl.ANY)] * 3,
+            out_specs=[hbm] * 3,
+            scratch_shapes=[dma((3,))],
+            compiler_params=pltpu.CompilerParams(vmem_limit_bytes=2**20),
+        )(*grads)
 
     in_specs = (
         P("pipe", "dp", None, "tensor"),

time: 56.4 us -> 51.6 us (0.915)
  the two profiles are of different devices: /device:TPU:1 before, /device:TPU:70 now
where the time goes in v2:
time: 51.6 us; the launch traced here: 51.5 us
  Pallas kernels  50.9 us (99%)
  between operations  0.64 us (1%)
    pallas_call x1, Pallas kernels, on_device(): pl.pallas_call(functools.partial(kernel, sizes), out_shape=(pltpu.VMEM((1...  49.7 us
    pallas_call x1, Pallas kernels, on_device(): pl.pallas_call(write_out, out_shape=[jax.ShapeDtypeStruct(g.shape, g.dtyp...  1.16 us

profile of v2, /device:TPU:70, one launch (start us, length us, event | category | flops | bytes accessed | tf_op | source)
XLA Modules:
  0.0 51.5 jit_solution(16747123214568451877)
XLA Ops:
  0.6 49.7 %shard_map.67 = (bf16[1,1,864,128]{3,2,1,0:T(8,128)(2,1)S(1)}, bf16[1,1,864,128]{3,2,1,0:T(8,128)(2,1)S(1)}, bf16[1,864,640]{2,1,0:T(8,128)(2,1)S(1)}) custom-call(bf16[1,1,160,128]{3,2,1,0:T(8,128)(2,1)} %bitcast.1, bf16[1,1,864,128]{3,2,1,0:T(8,128)(2,1)} %gate_hbm.1, bf16[1,1,864,128]{3,2,1,0:T(8,128)(2,1)} %up_hbm.1, bf16[1,864,2560]{2,1,0:T(8,128)(2,1)} %weight_hbm.1), custom_call_target="tpu_custom_call" | custom-call | tf_op jit(solution)/shard_map/pallas_call | solution.py:359
  50.3 1.2 %shard_map.68 = (bf16[1,1,864,128]{3,2,1,0:T(8,128)(2,1)}, bf16[1,1,864,128]{3,2,1,0:T(8,128)(2,1)}, bf16[1,864,640]{2,1,0:T(8,128)(2,1)}) custom-call(bf16[1,1,864,128]{3,2,1,0:T(8,128)(2,1)S(1)} %get-tuple-element.6.gg, bf16[1,1,864,128]{3,2,1,0:T(8,128)(2,1)S(1)} %get-tuple-element.7.ug, bf16[1,864,640]{2,1,0:T(8,128)(2,1)S(1)} %get-tuple-element.8.wg), custom_call_target="tpu_custom_call" | custom-call | tf_op jit(solution)/shard_map/pallas_call | solution.py:391

commit v3 on v2

--- a/solution.py
+++ b/solution.py
@@ -8,7 +8,8 @@
 from jax.sharding import PartitionSpec as P
 
 MESH = pl.DeviceIdType.MESH
-CHUNKS = 3
+PIECES = (9, 9, 9, 9, 9, 9)
+CHUNKS = len(PIECES) // 2
 
 
 def kernel(
@@ -33,8 +34,12 @@
     u_sib = u + 1 - 2 * core
     u_near = u + 2 - 4 * (u // 2)
     u_far = u_near + 1 - 2 * core
-    step = rows // CHUNKS
-    half = step // 2
+    unit = rows // sum(PIECES)
+    starts = [unit * sum(PIECES[:i]) for i in range(len(PIECES) + 1)]
+    tile = rows // 6
+
+    def span(first, count=1):
+        return pl.ds(starts[first], starts[first + count] - starts[first])
 
     loads = [
         pltpu.make_async_copy(og_hbm.at[0, 0], og_in, local_sem.at[0]),
@@ -86,13 +91,13 @@
     loads[2].wait()
 
     def hidden_rows(i, carry):
-        at = pl.ds(pl.multiple_of(i * half, half), half)
+        at = pl.ds(pl.multiple_of(i * tile, tile), tile)
         g = gate[at, :].astype(jnp.float32)
         v = up[at, :].astype(jnp.float32)
         hid[0, 0, at, :] = (g * jax.nn.sigmoid(g) * v).astype(jnp.bfloat16)
         return carry
 
-    lax.fori_loop(0, 2 * CHUNKS, hidden_rows, 0)
+    lax.fori_loop(0, rows // tile, hidden_rows, 0)
 
     pl.semaphore_wait(barrier, len(level) + u // 2 + zr)
 
@@ -126,14 +131,14 @@
     def send_hid(q, k, q_to, k_to, first, count, device):
         n = hid_count[0]
         hid_count[0] += 1
-        at = pl.ds(first * half, count * half)
+        at = span(first, count)
         send(
             hid.at[q, k, at], hid.at[q_to, k_to, at],
             hid_send.at[n], hid_recv.at[q_to, k_to, first], device,
         )
 
     def wait_hid(q, k, first, count):
-        at = pl.ds(first * half, count * half)
+        at = span(first, count)
         remote(
             hid.at[q, k, at], hid.at[q, k, at],
             hid_send.at[0], hid_recv.at[q, k, first], sib,
@@ -244,7 +249,8 @@
     take(2, together)
     take(1, apart)
     relay_mirror(0)
-    relay_ring(0, 2)
+    for c in range(2, CHUNKS):
+        relay_ring(0, c)
     offer(2, apart)
     take(-3)
     take(3, together)
@@ -252,8 +258,9 @@
     relay_mirror(1)
     take(2, apart)
     offer(3, apart)
-    relay_ring(1, 1)
-    relay_mirror(2)
+    for c in range(2, CHUNKS):
+        relay_ring(1, c - 1)
+        relay_mirror(c)
     take(3, apart)
     relay_block(0, u)
     for r in range(n_class):
@@ -270,7 +277,7 @@
     loads[3].wait()
 
     def projection_rows(i, carry):
-        at = pl.ds(pl.multiple_of(i * half, half), half)
+        at = pl.ds(pl.multiple_of(i * tile, tile), tile)
         grad = jnp.dot(
             weight[at, :], og_all[...].reshape(n_tensor * width, tok),
             preferred_element_type=jnp.float32,
@@ -282,9 +289,9 @@
         ug[0, 0, at, :] = (grad * g * s).astype(jnp.bfloat16)
         return carry
 
-    lax.fori_loop(0, 2 * CHUNKS, projection_rows, 0)
-
-    relay_ring(1, 2)
+    lax.fori_loop(0, rows // tile, projection_rows, 0)
+
+    relay_ring(1, CHUNKS - 1)
     relay_block(1, u_near)
 
     for k in range(1, n_dp):
@@ -306,11 +313,11 @@
         )
 
     def own_rows(i, carry):
-        at = pl.ds(pl.multiple_of(i * half, half), half)
+        at = pl.ds(pl.multiple_of(i * tile, tile), tile)
         acc[at, :] = term(0, at)
         return carry
 
-    lax.fori_loop(0, 2 * CHUNKS, own_rows, 0)
+    lax.fori_loop(0, rows // tile, own_rows, 0)
 
     for k in range(n_dp):
         wait_wog(1, k, u_sib)
@@ -320,12 +327,9 @@
         wait_hid(1, 2, 2 * c, 1)
         wait_hid(1, 2, 2 * c + 1, 1)
 
-        def mirror_rows(i, carry):
-            at = pl.ds(pl.multiple_of(i * half, half), half)
+        for piece in (2 * c, 2 * c + 1):
+            at = span(piece)
             wg[0, at, :] = ((acc[at, :] + term(1, at)) * scale).astype(jnp.bfloat16)
-            return carry
-
-        lax.fori_loop(2 * c, 2 * c + 2, mirror_rows, 0)
 
     for copy in sent:
         copy.wait_send()
@@ -380,7 +384,7 @@
                 dma((2, 7)),
                 dma((24,)),
                 dma((2, n_dp, 4)),
-                dma((36,)),
+                dma((12 * CHUNKS,)),
                 dma((2, n_dp, 2 * CHUNKS)),
                 pltpu.SemaphoreType.REGULAR((5,)),
             ],

time: 51.6 us -> 51.2 us (level)
  no operation moved by 1% of the time
where the time goes in v3:
time: 51.2 us; the launch traced here: 51 us
  Pallas kernels  50.4 us (98%)
  between operations  0.64 us (1%)
    pallas_call x1, Pallas kernels, on_device(): pl.pallas_call(functools.partial(kernel, sizes), out_shape=(pltpu.VMEM((1...  49.2 us
    pallas_call x1, Pallas kernels, on_device(): pl.pallas_call(write_out, out_shape=[jax.ShapeDtypeStruct(g.shape, g.dtyp...  1.16 us

profile of v3, /device:TPU:70, one launch (start us, length us, event | category | flops | bytes accessed | tf_op | source)
XLA Modules:
  0.0 51.0 jit_solution(2715603610847451164)
XLA Ops:
  0.6 49.2 %shard_map.67 = (bf16[1,1,864,128]{3,2,1,0:T(8,128)(2,1)S(1)}, bf16[1,1,864,128]{3,2,1,0:T(8,128)(2,1)S(1)}, bf16[1,864,640]{2,1,0:T(8,128)(2,1)S(1)}) custom-call(bf16[1,1,160,128]{3,2,1,0:T(8,128)(2,1)} %bitcast.1, bf16[1,1,864,128]{3,2,1,0:T(8,128)(2,1)} %gate_hbm.1, bf16[1,1,864,128]{3,2,1,0:T(8,128)(2,1)} %up_hbm.1, bf16[1,864,2560]{2,1,0:T(8,128)(2,1)} %weight_hbm.1), custom_call_target="tpu_custom_call" | custom-call | tf_op jit(solution)/shard_map/pallas_call | solution.py:363
  49.9 1.2 %shard_map.68 = (bf16[1,1,864,128]{3,2,1,0:T(8,128)(2,1)}, bf16[1,1,864,128]{3,2,1,0:T(8,128)(2,1)}, bf16[1,864,640]{2,1,0:T(8,128)(2,1)}) custom-call(bf16[1,1,864,128]{3,2,1,0:T(8,128)(2,1)S(1)} %get-tuple-element.6.gg, bf16[1,1,864,128]{3,2,1,0:T(8,128)(2,1)S(1)} %get-tuple-element.7.ug, bf16[1,864,640]{2,1,0:T(8,128)(2,1)S(1)} %get-tuple-element.8.wg), custom_call_target="tpu_custom_call" | custom-call | tf_op jit(solution)/shard_map/pallas_call | solution.py:395
